TPU v7x, 256 devices: a whole 4x4x8 slice. The times are simulated.
256 devices in a mesh: tile: 64 (over y_hi, x, z), head: 4 (over y_lo, core).
Axes of the slice: x: 4, y: 4 (y_hi: 2, y_lo: 2; y = y_hi * 2 + y_lo), z: 8, core: 2. Of those that a mesh axis runs over, the one named last changes fastest.
Arguments:
- tokens: bfloat16 [4, 96, 768, 512], P(None, 'head', 'tile'), may hold values from -6 to 6
- land_sea: int32 [96, 768], P('head', 'tile'), may hold values 0 or 1
- land_embed: float32 [2, 512], replicated, may hold values from -6 to 6
- gain_attn: float32 [512], replicated, may hold values from 0.1 to 1.9
- qkv_weight: bfloat16 [3, 512, 512], P(None, None, 'head'), may hold values from -0.25 to 0.25
- out_weight: bfloat16 [512, 512], P('head'), may hold values from -0.25 to 0.25
- bias_left: bfloat16 [8, 144, 32], P('head'), may hold values from -10 to 10
- bias_right: bfloat16 [8, 144, 32], P('head'), may hold values from -10 to 10
- gain_mlp: float32 [512], replicated, may hold values from 0.1 to 1.9
- up_weight: bfloat16 [512, 2048], replicated, may hold values from -0.25 to 0.25
- down_weight: bfloat16 [2048, 512], replicated, may hold values from -0.125 to 0.125
Outputs:
- block_out: bfloat16 [4, 96, 768, 512], P(None, 'head', 'tile')
All inputs are finite; a program needn't handle non-finite values. No bound on the sum of `land_sea` on one device may be relied on, other than what follows from the above.
Results may differ from a plain program's by a relative error of at most 0.011.
Values may be sent and summed in bfloat16 or wider, within the bound.
No kernel may reach another device: no remote copies, remote signals or barrier semaphores. Data moves between devices by JAX's collectives and lax.ppermute only.
A program may use at most 128 MiB of HBM per device.

v0:
```python
import jax
import jax.numpy as jnp
from jax import lax
from jax.sharding import PartitionSpec as P

HS = 64
WLV = 2
WLAT = 6
WLON = 12
LEVELS = 4


def from_behind(value, axis, steps):
    count = lax.axis_size(axis)
    pairs = [(source, (source + steps) % count) for source in range(count)]
    return lax.ppermute(value, axis, pairs)


def layer_norm(values, norm_gain):
    average = jnp.mean(values, axis=-1, keepdims=True)
    centred = values - average
    variance = jnp.mean(centred * centred, axis=-1, keepdims=True)
    return centred * lax.rsqrt(variance + 1e-05) * norm_gain


def region_label(coords, extent, window):
    return (coords >= extent - window).astype(jnp.int32) + (coords >= extent - window // 2).astype(
        jnp.int32
    )


def to_windows(field_grid):
    level_count, row_count, col_count, features = field_grid.shape
    pieces = field_grid.reshape(
        level_count // WLV, WLV, row_count // WLAT, WLAT, col_count // WLON, WLON, features
    )
    return pieces.transpose(0, 2, 4, 1, 3, 5, 6).reshape(-1, WLV * WLAT * WLON, features)


def from_windows(blocks, level_count, row_count, col_count):
    features = blocks.shape[-1]
    pieces = blocks.reshape(
        level_count // WLV, row_count // WLAT, col_count // WLON, WLV, WLAT, WLON, features
    )
    return pieces.transpose(0, 3, 1, 4, 2, 5, 6).reshape(
        level_count, row_count, col_count, features
    )


def window_penalty(level_coords, lat_coords, lat_total, col_count):
    level_label = region_label(level_coords, LEVELS, WLV)
    lat_label = region_label(lat_coords, lat_total, WLAT)
    labels = level_label[:, None] * 3 + lat_label[None, :]
    labels = jnp.broadcast_to(labels[:, :, None, None], labels.shape + (col_count, 1))
    flattened = to_windows(labels)[:, :, 0]
    same = flattened[:, :, None] == flattened[:, None, :]
    return jnp.where(same, jnp.float32(0.0), jnp.float32(-1000000000.0))


def project_qkv(row_grid, qkv_weight):
    product = jnp.einsum(
        "abcd,tde->tabce", row_grid, qkv_weight, preferred_element_type=jnp.float32
    )
    scaling = jnp.array([float(HS) ** (-0.5), 1.0, 1.0], jnp.float32)
    return (product * scaling[:, None, None, None, None]).astype(jnp.bfloat16)


def attend(qkv_grid, bias_left, bias_right, penalty, out_weight):
    query_block = to_windows(qkv_grid[0])
    key_block = to_windows(qkv_grid[1])
    value_block = to_windows(qkv_grid[2])
    head_count = bias_left.shape[0]
    head_dim = query_block.shape[-1] // head_count
    split_shape = query_block.shape[:2] + (head_count, head_dim)
    scores = jnp.einsum(
        "wqhe,wkhe->whqk",
        query_block.reshape(split_shape),
        key_block.reshape(split_shape),
        preferred_element_type=jnp.float32,
    )
    position_bias = jnp.einsum(
        "hqr,hkr->hqk", bias_left, bias_right, preferred_element_type=jnp.float32
    )
    scores = scores + position_bias[None] + penalty[:, None]
    highest = jnp.max(scores, axis=-1, keepdims=True)
    weights = jnp.exp(scores - highest)
    normed_weights = (weights / jnp.sum(weights, axis=-1, keepdims=True)).astype(jnp.bfloat16)
    blended = jnp.einsum(
        "whqk,wkhe->wqhe",
        normed_weights,
        value_block.reshape(split_shape),
        preferred_element_type=jnp.float32,
    ).astype(jnp.bfloat16)
    return jnp.dot(
        blended.reshape(query_block.shape), out_weight, preferred_element_type=jnp.float32
    )


def shards(
    tokens,
    land_sea,
    land_embed,
    gain_attn,
    qkv_weight,
    out_weight,
    bias_left,
    bias_right,
    gain_mlp,
    up_weight,
    down_weight,
):
    level_count, row_count, col_count, features = tokens.shape
    half_lon = WLON // 2
    half_lat = WLAT // 2
    embed_rows = jnp.where(land_sea[None, :, :, None] == 1, land_embed[1], land_embed[0])
    resid = tokens.astype(jnp.float32) + embed_rows
    normed = layer_norm(resid, gain_attn).astype(jnp.bfloat16)
    arriving = from_behind(normed[:, :, :half_lon], "tile", -1)
    lon_rolled = jnp.concatenate((normed[:, :, half_lon:], arriving), axis=2)
    level_coords = jnp.arange(level_count, dtype=jnp.int32)
    qkv_grid = project_qkv(lax.all_gather(lon_rolled, "head", axis=1, tiled=True), qkv_weight)
    qkv_grid = jnp.roll(qkv_grid, (-1, -half_lat), axis=(1, 2))
    lat_total = qkv_grid.shape[2]
    penalty = window_penalty(
        level_coords, jnp.arange(lat_total, dtype=jnp.int32), lat_total, col_count
    )
    partial_out = attend(qkv_grid, bias_left, bias_right, penalty, out_weight)
    partial_grid = jnp.roll(
        from_windows(partial_out, level_count, lat_total, col_count), (1, half_lat), axis=(0, 1)
    )
    attended = lax.psum_scatter(
        partial_grid.astype(jnp.bfloat16), "head", scatter_dimension=1, tiled=True
    ).astype(jnp.float32)
    behind = from_behind(
        attended[:, :, col_count - half_lon :].astype(jnp.bfloat16), "tile", 1
    ).astype(jnp.float32)
    attended = jnp.concatenate((behind, attended[:, :, : col_count - half_lon]), axis=2)
    mixed_resid = (resid + attended).reshape(-1, features)
    second = layer_norm(mixed_resid, gain_mlp).astype(jnp.bfloat16)
    hidden = jax.nn.gelu(
        jnp.dot(second, up_weight, preferred_element_type=jnp.float32), approximate=False
    ).astype(jnp.bfloat16)
    block_out = mixed_resid + jnp.dot(hidden, down_weight, preferred_element_type=jnp.float32)
    return block_out.astype(jnp.bfloat16).reshape(tokens.shape)


def solution(mesh):
    in_specs = (
        P(None, "head", "tile", None),
        P("head", "tile"),
        P(),
        P(),
        P(None, None, "head"),
        P("head", None),
        P("head", None, None),
        P("head", None, None),
        P(),
        P(),
        P(),
    )
    out_specs = P(None, "head", "tile", None)
    return jax.shard_map(shards, mesh=mesh, in_specs=in_specs, out_specs=out_specs, check_vma=False)
```

profile of v0, /device:TPU:1, one launch (start us, length us, event | category | flops | bytes accessed | tf_op | source)
XLA Modules:
  0.0 336.7 jit_solution(7166537341338922708)
XLA Ops:
  6.5 0.9 fusion.78
  7.4 0.8 broadcast_compare_fusion
  8.2 0.1 broadcast_select_fusion
  8.3 1.8 fusion.28
  10.1 1.8 multiply_reduce_fusion.1
  12.0 1.2 multiply_convert_fusion.4
  13.2 0.1 fusion.77
  13.3 11.3 %collective-permute-start = (bf16[4,24,6,512]{3,1,2,0:T(8,128)(2,1)S(1)}, bf16[4,24,6,512]{3,1,2,0:T(8,128)(2,1)S(1)}, u32[]{:S(2)}, u32[]{:S(2)}) collective-permute-start(bf16[4,24,6,512]{3,1,2,0:T(8,128)(2,1)S(1)} %get-tuple-element.13), channel_id=1, source_target_pairs={{0,252},{4,0},{8,4},{12,8},{16,12},{20,16},{24,20},{28,24},{32,28}... | collective-permute-start | bytes 1769480 | tf_op jit(solution)/shard_map/ppermute | solution.py:16
  24.6 12.0 %collective-permute-done = bf16[4,24,6,512]{3,1,2,0:T(8,128)(2,1)S(1)} collective-permute-done((bf16[4,24,6,512]{3,1,2,0:T(8,128)(2,1)S(1)}, bf16[4,24,6,512]{3,1,2,0:T(8,128)(2,1)S(1)}, u32[]{:S(2)}, u32[]{:S(2)}) %collective-permute-start) | collective-permute-done | bytes 589856 | tf_op jit(solution)/shard_map/ppermute | solution.py:16
  36.6 1.1 pad_maximum_fusion.3
  37.7 0.2 reduce-scatter.4.cloned.1.call-start
  38.0 0.1 broadcast_add_fusion
  38.1 0.1 eq.28
  38.3 0.1 copy.53
  38.3 1.7 fusion.80
  40.1 2.9 compare_select_fusion
  42.9 48.6 %all-gather.2.cloned.1.call-done = bf16[4,96,12,512]{3,1,2,0:T(8,128)(2,1)} async-done(((bf16[4,24,12,512]{3,1,2,0:T(8,128)(2,1)}), bf16[4,96,12,512]{3,1,2,0:T(8,128)(2,1)}) %all-gather.2.cloned.1.call-update) | async-done | bytes 4718608 | tf_op jit(solution)/shard_map/all_gather | solution.py:121
  91.6 5.0 %fusion.18 = bf16[3,4,96,12,128]{4,2,0,3,1:T(8,128)(2,1)S(1)} fusion(f32[3]{0:T(128)S(1)} %copy-done.8, bf16[4,96,12,512]{3,1,2,0:T(8,128)(2,1)} %all-gather.2.cloned.1.call-done, bf16[3,512,128]{2,1,0:T(8,128)(2,1)} %param.16), kind=kOutput, calls=%fused_computation.35 | convolution fusion | flops 1815478272 | bytes 8650764 | tf_op jit(solution)/shard_map/abcd,tde->tabce/dot_general | solution.py:61
  96.6 0.2 slice.82
  96.8 0.1 slice.83
  96.9 1.1 slice_maximum_fusion
  98.0 0.9 fusion.19
  98.8 2.2 fusion.75
  101.1 0.9 copy.46
  102.0 1.5 copy.47
  103.5 5.2 %reshape_reshape.10 = bf16[32,144,2,64]{3,2,0,1:T(2,128)(2,1)} reshape(bf16[2,16,1,2,6,12,128]{6,1,0,5,4,3,2:T(8,128)(2,1)} %copy.47) | data formatting | bytes 2359296 | tf_op jit(solution)/shard_map/reshape;reshape | solution.py:77
  108.7 2.2 copy.48
  110.9 1.5 copy.49
  112.4 5.2 %reshape_reshape.11 = bf16[32,144,2,64]{3,2,0,1:T(2,128)(2,1)} reshape(bf16[2,16,1,2,6,12,128]{6,1,0,5,4,3,2:T(8,128)(2,1)} %copy.49) | data formatting | bytes 2359296 | tf_op jit(solution)/shard_map/reshape;reshape | solution.py:78
  117.5 2.2 copy.44
  119.7 1.5 copy.45
  121.2 5.4 %reshape_reshape.9 = bf16[32,144,2,64]{3,2,0,1:T(2,128)(2,1)} reshape(bf16[2,16,1,2,6,12,128]{6,1,0,5,4,3,2:T(8,128)(2,1)} %copy.45) | data formatting | bytes 2359296 | tf_op jit(solution)/shard_map/reshape;reshape | solution.py:91
  126.6 5.3 %fusion.24 = f32[32,2,144,144]{2,3,1,0:T(8,128)S(1)} fusion(bf16[32,144,2,64]{3,2,0,1:T(2,128)(2,1)} %reshape_reshape.11, bf16[32,144,2,64]{3,2,0,1:T(2,128)(2,1)} %reshape_reshape.10), kind=kOutput, calls=%fused_computation.43 | convolution fusion | flops 169869312 | bytes 7667712 | tf_op jit(solution)/shard_map/wqhe,wkhe->whqk/dot_general | solution.py:75
  131.9 8.5 %fusion.79 = (f32[32,2,144]{2,1,0:T(2,128)S(1)}, f32[32,2,144,144]{2,3,1,0:T(8,128)}) fusion(f32[32,2,144,144]{2,3,1,0:T(8,128)S(1)} %fusion.24, f32[32,144,144]{1,2,0:T(8,128)} %compare_select_fusion, f32[2,144,144]{1,2,0:T(8,128)} %fusion.80), kind=kOutput, calls=%fused_computation.114 | output fusion | flops 7962767 | bytes 13473792 | tf_op jit(solution)/shard_map/sub | solution.py:86
  140.4 8.2 %convert_bitcast_fusion = bf16[32,144,2,64]{1,3,2,0:T(8,128)(2,1)} fusion(f32[32,2,144,144]{2,3,1,0:T(8,128)} %get-tuple-element.17, f32[32,2,144]{2,1,0:T(2,128)S(1)} %get-tuple-element.16, bf16[32,144,2,64]{3,2,0,1:T(2,128)(2,1)} %reshape_reshape.9), kind=kOutput, calls=%fused_computation.54 | convolution fusion | flops 173113344 | bytes 7704576 | tf_op jit(solution)/shard_map/whqk,wkhe->wqhe/dot_general | solution.py:88
  148.6 6.4 %copy.57 = bf16[32,144,2,64]{3,2,0,1:T(2,128)(2,1)} copy(bf16[32,144,2,64]{1,3,2,0:T(8,128)(2,1)} %convert_bitcast_fusion) | data formatting | bytes 2359296 | tf_op jit(solution)/shard_map/convert_element_type | solution.py:93
  155.0 5.4 %reshape.136 = bf16[2,16,2,6,12,128]{5,1,0,4,3,2:T(8,128)(2,1)} reshape(bf16[32,144,2,64]{3,2,0,1:T(2,128)(2,1)} %copy.57) | data formatting | bytes 2359296 | tf_op jit(solution)/shard_map/reshape.56
  160.4 4.8 %convolution_bitcast_fusion = bf16[2,2,16,6,1,12,512]{6,2,5,3,1,0,4:T(8,128)(2,1)} fusion(bf16[2,16,2,6,12,128]{5,1,0,4,3,2:T(8,128)(2,1)} %reshape.136, bf16[128,512]{1,0:T(8,128)(2,1)S(1)} %copy-done.5), kind=kOutput, calls=%fused_computation.39 | convolution fusion | flops 603979776 | bytes 6029312 | tf_op jit(solution)/shard_map/dot_general | solution.py:94
  165.2 9.3 %copy.59 = bf16[2,2,16,6,1,12,512]{6,1,0,5,3,2,4:T(2,128)(2,1)} copy(bf16[2,2,16,6,1,12,512]{6,2,5,3,1,0,4:T(8,128)(2,1)} %convolution_bitcast_fusion) | data formatting | bytes 9437184 | tf_op jit(solution)/shard_map/transpose | solution.py:45
  174.6 11.6 %reshape.137 = bf16[4,96,12,512]{3,0,2,1:T(4,128)(2,1)} reshape(bf16[2,2,16,6,1,12,512]{6,1,0,5,3,2,4:T(2,128)(2,1)} %copy.59) | data formatting | bytes 9437184 | tf_op jit(solution)/shard_map/reshape | solution.py:45
  186.2 5.0 %slice.89 = bf16[1,96,12,512]{3,0,2,1:T(2,128)(2,1)S(1)} slice(bf16[4,96,12,512]{3,0,2,1:T(4,128)(2,1)} %reshape.137), slice={[3:4], [0:96], [0:12], [0:512]} | slice | bytes 2359296 | tf_op jit(solution)/shard_map/jit(_roll_static)/slice | solution.py:128
  191.2 0.2 maximum_convert_fusion
  191.4 4.7 %fusion.11 = bf16[4,93,12,512]{3,0,2,1:T(4,128)(2,1)S(1)} fusion(bf16[3,96,12,512]{3,0,2,1:T(4,128)(2,1)S(1)} %bitcast.67, bf16[1,96,12,512]{3,0,2,1:T(2,128)(2,1)S(1)} %slice.89), kind=kLoop, calls=%fused_computation.24 | loop fusion | flops 9142272 | bytes 9289728 | tf_op jit(solution)/shard_map/convert.4
  196.1 3.0 pad_maximum_fusion.1
  199.2 4.9 %copy.86 = bf16[4,96,12,512]{3,2,0,1:T(8,128)(2,1)} copy(bf16[4,96,12,512]{3,0,2,1:T(4,128)(2,1)S(1)} %pad_maximum_fusion.1) | data formatting | bytes 9437184
  204.1 7.6 %reshape.143 = bf16[96,24576]{1,0:T(8,128)(2,1)} reshape(bf16[96,4,12,512]{3,2,1,0:T(8,128)(2,1)} %bitcast.68) | data formatting | bytes 9437184
  211.7 53.1 %reduce-scatter.4.cloned.1.call-done = bf16[24,24576]{1,0:T(8,128)(2,1)} async-done(((bf16[96,24576]{1,0:T(8,128)(2,1)}), bf16[24,24576]{1,0:T(8,128)(2,1)}) %reduce-scatter.4.cloned.1.call-update) | async-done | bytes 1179664
  264.8 2.9 reshape.144
  267.7 2.0 fusion.76
  269.7 0.3 copy.73
  270.0 1.3 collective-permute-start.1
  271.4 0.3 copy.74
  271.7 18.9 %collective-permute-done.1 = bf16[4,24,6,512]{3,1,2,0:T(8,128)(2,1)S(1)} collective-permute-done((bf16[4,24,6,512]{3,1,2,0:T(8,128)(2,1)S(1)}, bf16[4,24,6,512]{3,1,2,0:T(8,128)(2,1)S(1)}, u32[]{:S(2)}, u32[]{:S(2)}) %collective-permute-start.1) | collective-permute-done | bytes 589856 | tf_op jit(solution)/shard_map/ppermute | solution.py:16
  290.6 0.5 fusion.74
  291.1 3.0 copy.61
  294.2 0.5 multiply_reduce_fusion
  294.7 0.1 copy.62
  294.8 0.1 copy.63
  294.9 0.1 rsqrt.21
  295.0 3.9 %reshape.138 = f32[1152,512]{1,0:T(8,128)} reshape(f32[4,24,12,512]{3,2,1,0:T(8,128)} %copy.61) | data formatting | bytes 4718592 | tf_op jit(solution)/shard_map/reshape | solution.py:138
  298.9 0.1 div.27
  299.0 26.1 %fusion.20 = bf16[1152,512]{1,0:T(8,128)(2,1)S(1)} fusion(f32[1152,512]{1,0:T(8,128)} %reshape.138, bf16[2048,512]{1,0:T(8,128)(2,1)S(1)} %copy-done, bf16[512,2048]{1,0:T(8,128)(2,1)} %param.21, f32[512]{0:T(512)S(1)} %copy-done.7, f32[1152]{0:T(1024)S(1)} %rsqrt.21, f32[1152]{0:T(1024)S(1)} %div.27), kind=kOutput, calls=%fused_computation.41 | convolution fusion | flops 4988731392 | bytes 7744512 | tf_op jit(solution)/shard_map/dot_general | solution.py:143
  325.2 1.3 reshape.139
  326.5 3.1 copy.64
  (28 shorter events, 0.2 us)
Async XLA Ops:
  6.5 292.5 %copy-start = (bf16[2048,512]{1,0:T(8,128)(2,1)S(1)}, bf16[2048,512]{1,0:T(8,128)(2,1)}, u32[]{:S(2)}) copy-start(bf16[2048,512]{1,0:T(8,128)(2,1)} %param.22) | copy-start | bytes 6291460
  6.5 5.5 %copy-start.2 = (bf16[4,24,12,512]{3,1,2,0:T(8,128)(2,1)S(1)}, bf16[4,24,12,512]{3,1,2,0:T(8,128)(2,1)}, u32[]{:S(2)}) copy-start(bf16[4,24,12,512]{3,1,2,0:T(8,128)(2,1)} %param.12) | copy-start | bytes 3538948
  6.5 85.0 %all-gather.2.cloned.1.call-start = ((), (), s32[]{:S(2)}) async-start(), calls=%async_computation.1 | async-start | bytes 5898240 | tf_op jit(solution)/shard_map/all_gather | solution.py:121
  8.3 3.7 %copy-start.3 = (f32[24,12,512]{2,0,1:T(8,128)}, f32[24,12,512]{2,0,1:T(8,128)S(1)}, u32[]{:S(2)}) copy-start(f32[24,12,512]{2,0,1:T(8,128)S(1)} %broadcast_select_fusion) | copy-start | bytes 1769476
  12.0 26.3 %copy-start.6 = (bf16[2,144,32]{1,2,0:T(8,128)(2,1)S(1)}, bf16[2,144,32]{1,2,0:T(8,128)(2,1)}, u32[]{:S(2)}) copy-start(bf16[2,144,32]{1,2,0:T(8,128)(2,1)} %param.18) | copy-start | bytes 55300
  13.3 78.3 %copy-start.8 = (f32[3]{0:T(128)S(1)}, f32[3]{0:T(128)}, u32[]{:S(2)}) copy-start(f32[3]{0:T(128)} %constant.93.clone) | copy-start | bytes 40
  13.3 23.3 %collective-permute-start = (bf16[4,24,6,512]{3,1,2,0:T(8,128)(2,1)S(1)}, bf16[4,24,6,512]{3,1,2,0:T(8,128)(2,1)S(1)}, u32[]{:S(2)}, u32[]{:S(2)}) collective-permute-start(bf16[4,24,6,512]{3,1,2,0:T(8,128)(2,1)S(1)} %get-tuple-element.13), channel_id=1, source_target_pairs={{0,252},{4,0},{8,4},{12,8},{16,12},{20,16},{24,20},{28,24},{32,28}... | collective-permute-start | bytes 1769480 | tf_op jit(solution)/shard_map/ppermute | solution.py:16
  37.7 227.0 %reduce-scatter.4.cloned.1.call-start = ((), (), s32[]{:S(2)}) async-start(), calls=%async_computation.2 | async-start | bytes 5898240
  148.6 11.9 %copy-start.5 = (bf16[128,512]{1,0:T(8,128)(2,1)S(1)}, bf16[128,512]{1,0:T(8,128)(2,1)}, u32[]{:S(2)}) copy-start(bf16[128,512]{1,0:T(8,128)(2,1)} %param.17) | copy-start | bytes 393220
  186.2 5.0 %copy-start.1 = (bf16[4,96,12,512]{3,0,2,1:T(4,128)(2,1)S(1)}, bf16[4,96,12,512]{3,0,2,1:T(4,128)(2,1)}, u32[]{:S(2)}) copy-start(bf16[4,96,12,512]{3,0,2,1:T(4,128)(2,1)} %reshape.137) | copy-start | bytes 14155780
  267.7 22.9 %copy-start.4 = (f32[24,12,512]{2,0,1:T(8,128)S(1)}, f32[24,12,512]{2,0,1:T(8,128)}, u32[]{:S(2)}) copy-start(f32[24,12,512]{2,0,1:T(8,128)} %copy-done.3) | copy-start | bytes 1769476
  270.0 20.6 %collective-permute-start.1 = (bf16[4,24,6,512]{3,1,2,0:T(8,128)(2,1)S(1)}, bf16[4,24,6,512]{3,1,2,0:T(8,128)(2,1)S(1)}, u32[]{:S(2)}, u32[]{:S(2)}) collective-permute-start(bf16[4,24,6,512]{3,1,2,0:T(8,128)(2,1)S(1)} %copy.73), channel_id=1, source_target_pairs={{0,4},{4,8},{8,12},{12,16},{16,20},{20,24},{24,28},{28,32},{32,36}... | collective-permute-start | bytes 1769480 | tf_op jit(solution)/shard_map/ppermute | solution.py:16
  294.2 4.8 %copy-start.7 = (f32[512]{0:T(512)S(1)}, f32[512]{0:T(512)}, u32[]{:S(2)}) copy-start(f32[512]{0:T(512)} %param.20) | copy-start | bytes 6148
Sparse Core Ops, SparseCore 0:
  37.9 53.6 all-gather.1
  211.8 52.9 reduce-scatter.3
where the time goes:
time: 340 us; the launch traced here: 337 us
  waiting for transfers between devices  133 us (39%)
  local copies, waits for them, and re-layouts  96.9 us (28%)
  matrix products  51.2 us (15%)
  other arithmetic  29.1 us (9%)
  between operations  14 us (4%)
  starting transfers between devices  12.9 us (4%)
    unnamed x3, waiting for transfers between devices  53.1 us
    all_gather x1, waiting for transfers between devices, shards(): lax.all_gather(lon_rolled, 'head', axis=1, tiled=True)  48.6 us
    ppermute x2, waiting for transfers between devices, from_behind(): return lax.ppermute(value, axis, pairs)  30.9 us
    dot_general x1, matrix products, shards(): jnp.dot(hidden, down_weight, preferred_element_type=jnp.float32)  26.1 us
    unnamed x23, local copies, waits for them, and re-layouts  16.1 us
    ppermute x2, starting transfers between devices, from_behind(): return lax.ppermute(value, axis, pairs)  12.7 us
    reshape x1, local copies, waits for them, and re-layouts, from_windows(): pieces.transpose(0, 3, 1, 4, 2, 5, 6)  11.6 us
    transpose x1, local copies, waits for them, and re-layouts, from_windows(): pieces.transpose(0, 3, 1, 4, 2, 5, 6)  9.33 us
  transfers between devices with their start and end apart: 4, of which 4 were waited for; matrix products, arithmetic and copies ran while one was open for 2% of the time, Pallas kernels for 0%

commit v1 on v0

v1 whole, which is shorter than its diff:
```python
import functools

import jax
import jax.numpy as jnp
import numpy as np
from jax import lax
from jax.experimental import pallas as pl
from jax.experimental.pallas import tpu as pltpu
from jax.sharding import PartitionSpec as P

D = 512
AXES = ("tile", "head")
BF = jnp.bfloat16
F32 = jnp.float32
MIB = 2**20
PLACE = {1: (0, 0), 2: (0, 1), 3: (1, 0), 0: (1, 1)}
NT = (((1,), (1,)), ((), ()))
PENALTY = -1000000000.0
VMEM = pl.BlockSpec(memory_space=pltpu.VMEM)
SMEM = pl.BlockSpec(memory_space=pltpu.SMEM)
ANY = pl.BlockSpec(memory_space=pl.ANY)
HBM = pl.BlockSpec(memory_space=pltpu.HBM)


def dot(left, right):
    return jnp.dot(left, right, preferred_element_type=F32)


def dot_nt(left, right):
    return lax.dot_general(left, right, NT, preferred_element_type=F32)


def layer_norm(values, norm_gain):
    average = jnp.mean(values, axis=-1, keepdims=True)
    centred = values - average
    variance = jnp.mean(centred * centred, axis=-1, keepdims=True)
    return centred * lax.rsqrt(variance + 1e-05) * norm_gain


def front_kernel(
    wqkv, wo, left, right, tokens_in, land_in, embed_in, gain_in, gain_mlp_in,
    up_out, down_out, whole_out, norm_b_out, norm_a_out, resid_b_out, resid_a_out, gain_mlp_out,
    whole, factors, tokens, land, embed, gain, gain_mlp, norm, resid, sems,
):
    parity = lax.rem(lax.axis_index("tile"), 2)
    copies = []

    def copy(source, target):
        copies.append(pltpu.make_async_copy(source, target, sems.at[len(copies)]))
        copies[-1].start()
        return copies[-1]

    small = [
        copy(*pair) for pair in (
            (land_in, land), (embed_in, embed), (gain_in, gain), (gain_mlp_in, gain_mlp),
            (left, factors.at[0]), (right, factors.at[1]),
        )
    ]
    packed = [copy(wqkv, whole.at[:1536])]
    for block in range(4):
        lanes = pl.ds(128 * block, 128)
        packed.append(copy(wo.at[:, lanes], whole.at[pl.ds(1536 + 128 * block, 128)]))
    loads = [copy(tokens_in.at[:, 1 - parity], tokens.at[1]), copy(tokens_in.at[:, parity], tokens.at[0])]
    for one in small:
        one.wait()
    for index in range(2):
        base = 2048 + 128 * index
        whole[base : base + 64, :] = factors[index, :, :128]
        whole[base + 64 : base + 128, :] = jnp.concatenate(
            (factors[index, :, 128:], jnp.zeros((64, 112), BF)), axis=1
        )
    for one in packed:
        one.wait()
    stores = [
        copy(whole.at[:1152], up_out), copy(whole.at[1152:], down_out), copy(whole, whole_out),
        copy(gain_mlp, gain_mlp_out),
    ]
    eye = lax.broadcasted_iota(jnp.int32, (24, 24), 0) == lax.broadcasted_iota(jnp.int32, (24, 24), 1)
    columns = dot_nt(eye.astype(F32), land[...].astype(F32))
    sea_row, land_row = embed[0:1, :], embed[1:2, :]
    for half in (1, 0):
        side = parity if half == 0 else 1 - parity
        mine = jnp.where(side == 0, columns[:, :6], columns[:, 6:])
        loads[1 - half].wait()
        for col in range(6):
            added = jnp.where(mine[:, col : col + 1] > 0.5, land_row, sea_row)
            for level in range(4):
                pair, inner = PLACE[level]
                row = tokens[half, level, col].astype(F32) + added
                for k in range(3):
                    at = (pair * 3 + k) * 72 + inner * 36 + col * 6
                    resid[half, at : at + 6, :] = row[3 + 6 * k : 9 + 6 * k, :]
                at = 432 + pair * 40 + inner * 18 + col * 3
                resid[half, at : at + 3, :] = row[:3, :]
                resid[half, at + 80 : at + 83, :] = row[21:, :]
        for at in (468, 508, 548, 588):
            resid[half, at : at + 4, :] = jnp.zeros((4, D), F32)
        stores.append(copy(resid.at[half], (resid_a_out, resid_b_out)[half]))
        for start, count in ((0, 144), (144, 144), (288, 144), (432, 160)):
            rows = slice(start, start + count)
            norm[half, rows, :] = layer_norm(resid[half, rows, :], gain[...]).astype(BF)
        stores.append(copy(norm.at[half], (norm_a_out, norm_b_out)[half]))
    for one in stores:
        one.wait()


def block_rows(block):
    return (72 * block, 72) if block < 6 else (432 + 80 * (block - 6), 80)


def repeat4(value):
    return jnp.concatenate((value,) * 4, axis=0)


def head_stack(value, width):
    lane = lax.broadcasted_iota(jnp.int32, value.shape, 1) // width
    return jnp.concatenate(
        [jnp.where(lane == head, value, 0.0) for head in range(4)], axis=0
    ).astype(BF)


def head_pick(stacked):
    count = stacked.shape[0] // 4
    lane = lax.broadcasted_iota(jnp.int32, (count, stacked.shape[1]), 1) // 64
    total = stacked[:count]
    for head in range(1, 4):
        total = jnp.where(lane == head, stacked[count * head : count * head + count], total)
    return total


def qkv_kernel(
    group, norm_a, norm_b, pos_query, pos_key, *refs
):
    parts = refs[: 2 * (1 + group)]
    query, key, value, wkv, wo, bias_in, bias_edge, wq, left, right = refs[2 * (1 + group) :]

    def part(source, row, count):
        if group == 0:
            return parts[source][row : row + count, :]
        first, second = parts[2 * source : 2 * source + 2]
        if row + count <= 1152:
            return first[row : row + count, :]
        return second[row - 1152 : row - 1152 + count, :]

    for source in range(2):
        lanes = slice(128 * source, 128 * source + 128)
        wq[:, lanes] = part(source, 0, 512)
        wkv[:, lanes] = part(source, 512, 512)
        more = slice(256 + 128 * source, 384 + 128 * source)
        wkv[:128, more] = part(source, 1024, 128)
        wkv[128:, more] = part(source, 1152, 384)
        for block in range(4):
            wo[lanes, 128 * block : 128 * block + 128] = part(source, 1536 + 128 * block, 128)
        rows = slice(64 * source, 64 * source + 64)
        left[rows, :128] = part(source, 2048, 64)
        left[rows, 128:] = part(source, 2112, 64)
        right[rows, :128] = part(source, 2176, 64)
        right[rows, 128:] = part(source, 2240, 64)
    for half, norm in enumerate((norm_a, norm_b)):
        got_q = dot(norm[...], wq[...]) * 0.125
        got_kv = dot(norm[...], wkv[...])
        for block in range(8):
            at, count = block_rows(block)
            query[half, block, :count] = got_q[at : at + count].astype(BF)
            key[half, block, :count] = got_kv[at : at + count, :256].astype(BF)
            value[half, block, :count] = got_kv[at : at + count, 256:].astype(BF)
    factors = dot_nt(pos_query[...], left[...])
    q_level = lax.broadcasted_iota(jnp.int32, (72, 144), 0) >= 36
    k_level = lax.rem(lax.broadcasted_iota(jnp.int32, (72, 144), 1), 72) >= 36
    split = repeat4(jnp.where(q_level == k_level, 0.0, PENALTY))
    row = lax.broadcasted_iota(jnp.int32, (40, 160), 0)
    lane = lax.broadcasted_iota(jnp.int32, (40, 160), 1)
    slot = lax.rem(lane, 40)
    halo = lax.rem(lane // 40, 2) == 1
    head = lax.axis_index("head")
    for half in range(2):
        own_rows = head_stack(factors[72 * half : 72 * half + 72, :], 32)
        keys = dot_nt(right[...], pos_key[144 * half : 144 * half + 144, :]).astype(BF)
        bias = dot(own_rows, keys)
        bias_in[half, 0] = bias
        bias_in[half, 1] = bias + split
        for side in range(2):
            at = 144 + 80 * half + 40 * (1 - side)
            own_rows = head_stack(factors[at : at + 40, :], 32)
            at = 288 + 320 * half + 160 * side
            keys = dot_nt(right[...], pos_key[at : at + 160, :]).astype(BF)
            bias = dot(own_rows, keys)
            outside = jnp.logical_and(halo, head == 3 * side)
            hidden = jnp.logical_or(slot >= 36, outside)
            bias_edge[half, side, 0] = bias + repeat4(jnp.where(hidden, PENALTY, 0.0))
            hidden = jnp.logical_or(hidden, (row >= 18) != (slot >= 18))
            bias_edge[half, side, 1] = bias + repeat4(jnp.where(hidden, PENALTY, 0.0))


def attend(query, keys, values, bias):
    scores = dot_nt(head_stack(query, 64), keys) + bias[...]
    weights = jnp.exp(scores - jnp.max(scores, axis=-1, keepdims=True))
    scale = 1.0 / jnp.sum(weights, axis=-1, keepdims=True)
    return head_pick(dot(weights.astype(BF), values) * scale)


def fetch_kernel(up_in, down_in, after, up, down, sems):
    copies = (
        pltpu.make_async_copy(up_in, up, sems.at[0]),
        pltpu.make_async_copy(down_in, down, sems.at[1]),
    )
    for one in copies:
        one.start()
    for one in copies:
        one.wait()


def feed_forward(heads, resid, wo_0, wo_1, gain, up, down, hidden):
    mixed = resid + dot(heads[0].astype(BF), wo_0[...]) + dot(heads[1].astype(BF), wo_1[...])
    second = layer_norm(mixed, gain[...]).astype(BF)
    for start in range(0, 2048, 512):
        inner = dot(second, up[:, start : start + 512])
        inner = 0.5 * inner * (1.0 + lax.erf(inner * 0.7071067811865476))
        hidden[:, start : start + 512] = inner.astype(BF)
    return mixed + dot(hidden[...], down[...])


def half_kernel(half, remote, resid, gain, up, down, *refs):
    groups = (refs[:6], refs[6:12])
    out, edge_key, edge_value, keys, values, heads, hidden = refs[12:]
    for group, (query, key, value, wkv, wo, bias) in enumerate(groups):
        got = dot(remote[...], wkv[...])
        for lanes, near, target, edge in ((0, key, keys, edge_key), (256, value, values, edge_value)):
            for block in range(8):
                at, count = block_rows(block)
                part = got[at : at + count, lanes : lanes + 256]
                if block < 6:
                    joined = jnp.concatenate((near[half, block, :72].astype(F32), part), axis=0)
                    target[block] = joined.astype(BF)
                else:
                    edge[group, block - 6] = part.astype(BF)
        for block in range(6):
            heads[group, 72 * block : 72 * block + 72, :] = attend(
                query[half, block, :72].astype(F32), keys[block], values[block], bias.at[half, block // 3]
            )
    out[...] = feed_forward(
        heads, resid[:432, :], groups[0][4], groups[1][4], gain, up, down, hidden
    )


def gather_kernel(after, remote_b, norm_b, norm_a, remote_a, first, second):
    odd = lax.rem(lax.axis_index("head"), 2) == 1
    for index, block in enumerate((norm_a, norm_b, remote_b, remote_a)):
        rows = slice(80 * index, 80 * index + 80)
        top, bottom = block[432:512, :], block[512:592, :]
        first[rows, :] = jnp.where(odd, top, bottom)
        second[rows, :] = jnp.where(odd, bottom, top)


def edge_kernel(
    first, second, key_a, value_a, key_b, value_b, resid_a, resid_b, gain, out_a, out_b, up, down, *refs
):
    groups = (refs[:6], refs[6:12])
    out, halo, heads, edges, grid, stage, hidden, sems = refs[12:]
    parity = lax.rem(lax.axis_index("tile"), 2)
    odd = lax.rem(lax.axis_index("head"), 2)
    for group, (query, key, value, wkv, wo, bias) in enumerate(groups):
        halo[1 - odd] = dot(first[...], wkv[...])
        halo[odd] = dot(second[...], wkv[...])
        for half in range(2):
            remote = ((key_a, value_a), (key_b, value_b))[half]
            near, far = ((0, 240), (80, 160))[half]
            for side in range(2):
                own_query = query[half, 6 + side].astype(F32)
                own = [ref[half, 6 + side].astype(F32) for ref in (key, value)]
                other = [ref[group, side].astype(F32) for ref in remote]
                for pair in range(2):
                    rows = slice(40 * pair, 40 * pair + 40)
                    joined = []
                    for index in range(2):
                        lanes = slice(256 * index, 256 * index + 256)
                        parts = (
                            own[index][rows], halo[side, near + 40 * pair : near + 40 * pair + 40, lanes],
                            other[index][rows], halo[side, far + 40 * pair : far + 40 * pair + 40, lanes],
                        )
                        joined.append(jnp.concatenate(parts, axis=0).astype(BF))
                    got = attend(own_query[rows], joined[0], joined[1], bias.at[half, side, pair])
                    at = 144 * half + 72 * side + 36 * pair
                    heads[group, at : at + 36, :] = got[:36]
    here = [r[at : at + 36, :] for r in (resid_a, resid_b) for at in (432, 472, 512, 552)]
    for index, part in enumerate(here):
        edges[36 * index : 36 * index + 36, :] = part
    edges[...] = feed_forward(
        heads, edges[...], groups[0][4], groups[1][4], gain, up, down, hidden
    )
    copies = []
    for half, inside in enumerate((out_a, out_b)):
        place = parity if half == 0 else 1 - parity
        for level in range(4):
            pair, inner = PLACE[level]
            for col in range(6):
                at = 144 * half + pair * 36 + inner * 18 + col * 3
                grid[level, col, :3, :] = edges[at : at + 3, :]
                grid[level, col, 21:, :] = edges[at + 72 : at + 75, :]
                for k in range(3):
                    at = (pair * 3 + k) * 72 + inner * 36 + col * 6
                    grid[level, col, 3 + 6 * k : 9 + 6 * k, :] = inside[at : at + 6, :]
                stage[half, level, col] = grid[level, col].astype(BF)
            copies.append(
                pltpu.make_async_copy(stage.at[half, level], out.at[level, place], sems.at[4 * half + level])
            )
            copies[-1].start()
    for one in copies:
        one.wait()


def call(kernel, out_shape, in_specs, scratch=(), limit=16, flops=0, out_specs=None, **extra):
    many = isinstance(out_shape, (list, tuple))
    return pl.pallas_call(
        kernel,
        out_shape=out_shape,
        in_specs=in_specs,
        out_specs=out_specs or ([VMEM] * len(out_shape) if many else VMEM),
        scratch_shapes=scratch,
        compiler_params=pltpu.CompilerParams(vmem_limit_bytes=limit * MIB),
        cost_estimate=pl.CostEstimate(flops=flops, bytes_accessed=2 * MIB, transcendentals=0),
        **extra,
    )


def shape(*dims, dtype=BF):
    return jax.ShapeDtypeStruct(dims, dtype)


def position_tables():
    tables = []
    for parity in range(2):
        columns = (1 - parity, parity)

        def inside(half):
            c = columns[half]
            return [l * 72 + r * 12 + 6 * c + col for l in range(2) for col in range(6) for r in range(6)]

        def edge(half, rows):
            c = columns[half]
            spots = [
                l * 72 + (3 * rows + r) * 12 + 6 * c + col
                for l in range(2) for col in range(6) for r in range(3)
            ]
            return spots + [-1] * 4

        query = inside(0) + inside(1)
        for half in range(2):
            query += edge(half, 0) + edge(half, 1)
        key = []
        for half in range(2):
            key += inside(half) + inside(1 - half)
        for half in range(2):
            for side in range(2):
                near = 1 - side
                for h in (half, 1 - half):
                    key += edge(h, near) + edge(h, 1 - near)
        tables.append(query + key)
    return np.array(tables, np.int32)


def pairs_of(tiles, move):
    pairs = []
    for tile in range(tiles):
        for head in range(4):
            target = move(tile, head)
            if target is not None:
                pairs.append((tile * 4 + head, (target[0] % tiles) * 4 + target[1]))
    return pairs


def shards(
    tokens, land_sea, land_embed, gain_attn, qkv_weight, out_weight, bias_left, bias_right,
    gain_mlp, up_weight, down_weight,
):
    tiles = lax.axis_size("tile")
    parity = lax.rem(lax.axis_index("tile"), 2)

    def along_y(steps):
        def move(t, h):
            high, rest = divmod(t, tiles // 2)
            y = (2 * high + h // 2 + steps) % 4
            return (y // 2) * (tiles // 2) + rest, (y % 2) * 2 + h % 2

        return move

    def send(value, move):
        return lax.ppermute(value, AXES, pairs_of(tiles, move))

    swap_a = lambda t, h: (t + 1 if t % 2 else t - 1, h)
    swap_b = lambda t, h: (t ^ 1, h)
    swap_core = lambda t, h: (t, h ^ 1)
    swap_chip = lambda t, h: (t, 3 - h) if h in (1, 2) else None

    grid = tokens.transpose(0, 2, 1, 3).reshape(4, 2, 6, 24, D)
    rows = [shape(592, D)] * 2 + [shape(592, D, dtype=F32)] * 2
    pack_up, pack_down, pack, norm_b, norm_a, resid_b, resid_a, gain_mlp = call(
        front_kernel,
        [shape(1152, 128), shape(1152, 128), shape(2304, 128)] + rows + [shape(1, D, dtype=F32)],
        [HBM] * 9,
        [
            pltpu.VMEM((2304, 128), BF), pltpu.VMEM((2, 64, 144), BF), pltpu.VMEM((2, 4, 6, 24, D), BF),
            pltpu.VMEM((12, 24), jnp.int32), pltpu.VMEM((2, D), F32), pltpu.VMEM((1, D), F32),
            pltpu.VMEM((1, D), F32), pltpu.VMEM((2, 592, D), BF), pltpu.VMEM((2, 592, D), F32),
            pltpu.SemaphoreType.DMA((21,)),
        ],
        limit=63,
        out_specs=[HBM] * 8,
        name="front",
    )(
        qkv_weight.reshape(1536, 128),
        out_weight,
        bias_left.transpose(0, 2, 1).reshape(64, 144),
        bias_right.transpose(0, 2, 1).reshape(64, 144),
        grid, land_sea.transpose(1, 0), land_embed, gain_attn[None], gain_mlp[None],
    )
    far_up = send(pack_up, along_y(1))
    far_down = send(pack_down, along_y(-1))
    mate = send(pack, swap_core)

    remote_b = send(norm_b, swap_b)
    remote_a = send(norm_a, swap_a)
    fwd_up = send(far_up, swap_core)
    fwd_down = send(far_down, swap_core)

    places = jnp.asarray(position_tables())
    places = jnp.where(parity == 1, places[1], places[0])
    onehot = (places[:, None] == jnp.arange(256, dtype=jnp.int32)[None, :]).astype(BF)
    def run_qkv(group, parts):
        return call(
            functools.partial(qkv_kernel, group),
            [shape(2, 8, 80, 256)] * 3
            + [shape(D, 512), shape(256, D)]
            + [shape(2, 2, 288, 144, dtype=F32), shape(2, 2, 2, 160, 160, dtype=F32)],
            [VMEM] * (4 + len(parts)),
            [pltpu.VMEM((D, 256), BF)] + [pltpu.VMEM((128, 256), BF)] * 2,
            flops=2 * 10**9,
            name="qkv_" + str(group),
        )(norm_a, norm_b, onehot[:304], onehot[304:], *parts)

    near = run_qkv(0, (pack, mate))
    up, down = call(
        fetch_kernel, [shape(D, 2048), shape(2048, D)], [HBM] * 3,
        [pltpu.SemaphoreType.DMA((2,))], flops=10**9, name="fetch",
    )(up_weight, down_weight, near[3])
    far = run_qkv(1, (far_up, far_down, fwd_up, fwd_down))
    heads = near[:6] + far[:6]

    def run_half(half, remote, resid):
        return call(
            functools.partial(half_kernel, half),
            [shape(432, D, dtype=F32), shape(2, 2, 80, 256), shape(2, 2, 80, 256)],
            [VMEM] * 17,
            [
                pltpu.VMEM((6, 144, 256), BF), pltpu.VMEM((6, 144, 256), BF),
                pltpu.VMEM((2, 432, 256), F32), pltpu.VMEM((432, 2048), BF),
            ],
            flops=4 * 10**9,
            name="half_" + "ab"[half],
        )(remote, resid, gain_mlp, up, down, *heads)

    inner_b, key_b, value_b = run_half(1, remote_b, resid_b)
    first, second = call(
        gather_kernel, [shape(320, D)] * 2, [ANY] + [VMEM] * 4, name="gather"
    )(key_b, remote_b, norm_b, norm_a, remote_a)
    first = send(first, swap_core)
    second = send(second, swap_chip)
    inner_a, key_a, value_a = run_half(0, remote_a, resid_a)

    out = call(
        edge_kernel,
        shape(4, 2, 6, 24, D),
        [VMEM] * 25,
        [
            pltpu.VMEM((2, 320, 512), F32), pltpu.VMEM((2, 288, 256), F32), pltpu.VMEM((288, D), F32),
            pltpu.VMEM((4, 6, 24, D), F32), pltpu.VMEM((2, 4, 6, 24, D), BF), pltpu.VMEM((288, 2048), BF),
            pltpu.SemaphoreType.DMA((8,)),
        ],
        out_specs=ANY,
        flops=4 * 10**9,
        name="edge",
    )(
        first, second, key_a, value_a, key_b, value_b, resid_a, resid_b, gain_mlp, inner_a, inner_b,
        up, down, *near[:5], near[6], *far[:5], far[6],
    )
    return out.reshape(4, 12, 24, D).transpose(0, 2, 1, 3)


def solution(mesh):
    in_specs = (
        P(None, "head", "tile", None),
        P("head", "tile"),
        P(),
        P(),
        P(None, None, "head"),
        P("head", None),
        P("head", None, None),
        P("head", None, None),
        P(),
        P(),
        P(),
    )
    out_specs = P(None, "head", "tile", None)
    return jax.shard_map(shards, mesh=mesh, in_specs=in_specs, out_specs=out_specs, check_vma=False)
```

time: 340 us -> 47.9 us (0.14)
  waiting for transfers between devices: 133 us -> 2.95 us
  local copies, waits for them, and re-layouts: 96.9 us -> 0.09 us
  matrix products: 51.2 us -> 0 us
  other arithmetic: 29.1 us -> 0.25 us
  Pallas kernels: 0 us -> 25 us
  between operations: 14 us -> 0.44 us
  starting transfers between devices: 12.9 us -> 19.1 us
    unnamed x3 -> x0, waiting for transfers between devices: 53.1 us -> none
    dot_general x6 -> x0, matrix products: 51.2 us -> none  [the longest x1 26.1 us: shards(): jnp.dot(hidden, down_weight, preferred_element_type=jnp.float32)]
    all_gather x1 -> x0, waiting for transfers between devices: 48.6 us -> none  [shards(): lax.all_gather(lon_rolled, 'head', axis=1, tiled=True)]
    ppermute x2 -> x9, waiting for transfers between devices: 30.9 us -> 2.95 us  [send(): return lax.ppermute(value, AXES, pairs_of(tiles, move))]
    pallas_call x0 -> x8, Pallas kernels: none -> 25 us  [the longest x2 9.22 us: run_half(): call(functools.partial(half_kernel, half), [shape(432, D, dtype=F32), sha...]
    another operation x4 -> x0, local copies, waits for them, and re-layouts: 21.2 us -> none
    reshape x4 -> x0, local copies, waits for them, and re-layouts: 20 us -> none  [the longest x1 11.6 us: from_windows(): pieces.transpose(0, 3, 1, 4, 2, 5, 6)]
    unnamed x23 -> x20, local copies, waits for them, and re-layouts: 16.1 us -> 0.05 us
  transfers between devices with their start and end apart: 4 -> 9, of which waited for: 4 -> 2; matrix products, arithmetic and copies ran while one was open for 2% -> 1% of each run, Pallas kernels for 0% -> 32%
where the time goes in v1:
time: 47.9 us; the launch traced here: 47.8 us
  Pallas kernels  25 us (52%)
  starting transfers between devices  19.1 us (40%)
  waiting for transfers between devices  2.95 us (6%)
    ppermute x9, starting transfers between devices, send(): return lax.ppermute(value, AXES, pairs_of(tiles, move))  19.1 us
    pallas_call x2, Pallas kernels, run_half(): call(functools.partial(half_kernel, half), [shape(432, D, dtype=F32), sha...  9.22 us
    pallas_call x2, Pallas kernels, run_qkv(): call(functools.partial(qkv_kernel, group), [shape(2, 8, 80, 256)] * 3 + [...  5.93 us
    pallas_call x1, Pallas kernels, shards(): call(edge_kernel, shape(4, 2, 6, 24, D), [VMEM] * 25, [pltpu.VMEM((2, 320...  5.75 us
    pallas_call x1, Pallas kernels, shards(): call(front_kernel, [shape(1152, 128), shape(1152, 128), shape(2304, 128)]...  3.7 us
    ppermute x9, waiting for transfers between devices, send(): return lax.ppermute(value, AXES, pairs_of(tiles, move))  2.95 us
  transfers between devices with their start and end apart: 9, of which 2 were waited for; matrix products, arithmetic and copies ran while one was open for 1% of the time, Pallas kernels for 32%

profile of v1, /device:TPU:1, one launch (start us, length us, event | category | flops | bytes accessed | tf_op | source)
XLA Modules:
  0.0 47.8 jit_solution(11636225133390215505)
XLA Ops:
  0.0 0.0 copy-start.8
  0.0 0.0 copy-start.9
  0.0 3.7 %front.1 = (bf16[1152,128]{1,0:T(8,128)(2,1)}, bf16[1152,128]{1,0:T(8,128)(2,1)}, bf16[2304,128]{1,0:T(8,128)(2,1)}, bf16[592,512]{1,0:T(8,128)(2,1)}, bf16[592,...) custom-call(bf16[1536,128]{1,0:T(8,128)(2,1)} %bitcast.17, bf16[128,512]{1,0:T(8,128)(2,1)} %wo.1, ...), custom_call_target="tpu_custom_call" | custom-call | bytes 2097152 | tf_op jit(solution)/shard_map/front/pallas_call | solution.py:397
  3.7 0.0 copy-start.4
  3.7 0.0 copy-start.5
  3.7 0.0 copy-start.7
  3.7 2.2 %collective-permute-start.2 = (bf16[1152,128]{1,0:T(8,128)(2,1)}, bf16[1152,128]{1,0:T(8,128)(2,1)S(1)}, u32[]{:S(2)}, u32[]{:S(2)}) collective-permute-start(bf16[1152,128]{1,0:T(8,128)(2,1)} %get-tuple-element.50), channel_id=1, source_target_pairs={{0,2},{1,3},{2,128},{3,129},{4,6},{5,7},{6,132},{7,133},{8,10},{9,... | collective-permute-start | bytes 884744 | tf_op jit(solution)/shard_map/ppermute | solution.py:388
  5.9 1.5 %collective-permute-start.3 = (bf16[1152,128]{1,0:T(8,128)(2,1)}, bf16[1152,128]{1,0:T(8,128)(2,1)}, u32[]{:S(2)}, u32[]{:S(2)}) collective-permute-start(bf16[1152,128]{1,0:T(8,128)(2,1)} %get-tuple-element.51), channel_id=1, source_target_pairs={{0,130},{1,131},{2,0},{3,1},{4,134},{5,135},{6,4},{7,5},{8,138},{9... | collective-permute-start | bytes 884744 | tf_op jit(solution)/shard_map/ppermute | solution.py:388
  7.5 2.8 %collective-permute-start.1 = (bf16[2304,128]{1,0:T(8,128)(2,1)}, bf16[2304,128]{1,0:T(8,128)(2,1)}, u32[]{:S(2)}, u32[]{:S(2)}) collective-permute-start(bf16[2304,128]{1,0:T(8,128)(2,1)} %get-tuple-element.41.refs_0_), channel_id=1, source_target_pairs={{0,1},{1,0},{2,3},{3,2},{4,5},{5,4},{6,7},{7,6},{8,9},{9,8},{10,11... | collective-permute-start | bytes 1769480 | tf_op jit(solution)/shard_map/ppermute | solution.py:388
  10.3 0.0 collective-permute-start
  10.3 8.2 %collective-permute-start.6 = (bf16[592,512]{1,0:T(8,128)(2,1)}, bf16[592,512]{1,0:T(8,128)(2,1)S(1)}, u32[]{:S(2)}, u32[]{:S(2)}) collective-permute-start(bf16[592,512]{1,0:T(8,128)(2,1)} %get-tuple-element.40.norm_a), channel_id=1, source_target_pairs={{0,252},{1,253},{2,254},{3,255},{4,8},{5,9},{6,10},{7,11},{8,4},{9... | collective-permute-start | bytes 1818632 | tf_op jit(solution)/shard_map/ppermute | solution.py:388
  18.5 0.0 copy-done.8
  18.5 0.0 copy-done.9
  18.5 0.0 collective-permute-done.2.refs_0_
  18.5 0.6 %collective-permute-start.4 = (bf16[1152,128]{1,0:T(8,128)(2,1)S(1)}, bf16[1152,128]{1,0:T(8,128)(2,1)S(1)}, u32[]{:S(2)}, u32[]{:S(2)}) collective-permute-start(bf16[1152,128]{1,0:T(8,128)(2,1)S(1)} %collective-permute-done.2.refs_0_), channel_id=1, source_target_pairs={{0,1},{1,0},{2,3},{3,2},{4,5},{5,4},{6,7},{7,6},{8,9},{9,8},{10,11... | collective-permute-start | bytes 884744 | tf_op jit(solution)/shard_map/ppermute | solution.py:388
  19.2 0.0 collective-permute-done.3.refs_1_
  19.2 0.3 collective-permute-start.5
  19.5 0.2 fusion
  19.8 0.0 copy-start
  19.8 0.0 copy-start.1
  19.8 0.0 collective-permute-done.1.refs_1_
  19.8 0.0 copy-done.4
  19.8 0.0 copy-done.5
  19.8 0.0 copy-done.7
  19.8 3.0 %qkv_0.1 = (bf16[2,8,80,256]{3,2,1,0:T(8,128)(2,1)S(1)}, bf16[2,8,80,256]{3,2,1,0:T(8,128)(2,1)S(1)}, bf16[2,8,80,256]{3,2,1,0:T(8,128)(2,1)S(1)}, bf16[512,512]...) custom-call(bf16[592,512]{1,0:T(8,128)(2,1)S(1)} %copy-done.5, ...), custom_call_target="tpu_custom_call" | custom-call | flops 2000000000 | bytes 2097152 | tf_op jit(solution)/shard_map/qkv_0/pallas_call | solution.py:430
  22.9 0.0 copy-done
  22.9 0.0 copy-done.1
  22.9 0.3 fetch.1
  23.2 0.0 copy-start.2
  23.2 0.0 copy-start.6
  23.2 0.0 collective-permute-done.4.refs_2_
  23.2 0.0 collective-permute-done.5.refs_3_
  23.2 2.9 %qkv_1.1 = (bf16[2,8,80,256]{3,2,1,0:T(8,128)(2,1)S(1)}, bf16[2,8,80,256]{3,2,1,0:T(8,128)(2,1)S(1)}, bf16[2,8,80,256]{3,2,1,0:T(8,128)(2,1)S(1)}, bf16[512,512]...) custom-call(bf16[592,512]{1,0:T(8,128)(2,1)S(1)} %copy-done.5, ...), custom_call_target="tpu_custom_call" | custom-call | flops 2000000000 | bytes 2097152 | tf_op jit(solution)/shard_map/qkv_1/pallas_call | solution.py:430
  26.1 0.0 collective-permute-done.remote.remote_b
  26.1 0.0 copy-done.2
  26.2 0.0 copy-done.6
  26.2 4.6 %half_b.1 = (f32[432,512]{1,0:T(8,128)S(1)}, bf16[2,2,80,256]{3,2,1,0:T(8,128)(2,1)S(1)}, bf16[2,2,80,256]{3,2,1,0:T(8,128)(2,1)S(1)}) custom-call(bf16[592,512]{1,0:T(8,128)(2,1)S(1)} %collective-permute-done.remote.remote_b, f32[592,512]{1,0:T(8,128)S(1)} %copy-done.2, f32[1,512]{1,0:T(1,128)S(1)} %copy-done.6, ...), custom_call_target="tpu_custom_call" | custom-call | flops 4000000000 | bytes 2097152 | tf_op jit(solution)/shard_map/half_b/pallas_call | solution.py:450
  30.8 1.8 %collective-permute-done.6.remote_a.remote = bf16[592,512]{1,0:T(8,128)(2,1)S(1)} collective-permute-done((bf16[592,512]{1,0:T(8,128)(2,1)}, bf16[592,512]{1,0:T(8,128)(2,1)S(1)}, u32[]{:S(2)}, u32[]{:S(2)}) %collective-permute-start.6) | collective-permute-done | bytes 606240 | tf_op jit(solution)/shard_map/ppermute | solution.py:388
  32.5 0.0 copy-start.3
  32.5 0.1 gather.1
  32.6 0.9 %collective-permute-start.7 = (bf16[320,512]{1,0:T(8,128)(2,1)S(1)}, bf16[320,512]{1,0:T(8,128)(2,1)S(1)}, u32[]{:S(2)}, u32[]{:S(2)}) collective-permute-start(bf16[320,512]{1,0:T(8,128)(2,1)S(1)} %get-tuple-element.59), channel_id=1, source_target_pairs={{0,1},{1,0},{2,3},{3,2},{4,5},{5,4},{6,7},{7,6},{8,9},{9,8},{10,11... | collective-permute-start | bytes 983048 | tf_op jit(solution)/shard_map/ppermute | solution.py:388
  33.5 2.6 %collective-permute-start.8 = (bf16[320,512]{1,0:T(8,128)(2,1)S(1)}, bf16[320,512]{1,0:T(8,128)(2,1)S(1)}, u32[]{:S(2)}, u32[]{:S(2)}) collective-permute-start(bf16[320,512]{1,0:T(8,128)(2,1)S(1)} %get-tuple-element.60), channel_id=1, source_target_pairs={{1,2},{2,1},{5,6},{6,5},{9,10},{10,9},{13,14},{14,13},{17,18},{18,... | collective-permute-start | bytes 983048 | tf_op jit(solution)/shard_map/ppermute | solution.py:388
  36.0 0.0 copy-done.3
  36.0 4.6 %half_a.1 = (f32[432,512]{1,0:T(8,128)S(1)}, bf16[2,2,80,256]{3,2,1,0:T(8,128)(2,1)S(1)}, bf16[2,2,80,256]{3,2,1,0:T(8,128)(2,1)S(1)}) custom-call(bf16[592,512]{1,0:T(8,128)(2,1)S(1)} %collective-permute-done.6.remote_a.remote, f32[592,512]{1,0:T(8,128)S(1)} %copy-done.3, f32[1,512]{1,0:T(1,128)S(1)} %copy-done.6, ...), custom_call_target="tpu_custom_call" | custom-call | flops 4000000000 | bytes 2097152 | tf_op jit(solution)/shard_map/half_a/pallas_call | solution.py:450
  40.7 0.0 collective-permute-done.7.first
  40.7 1.2 %collective-permute-done.8.second = bf16[320,512]{1,0:T(8,128)(2,1)S(1)} collective-permute-done((bf16[320,512]{1,0:T(8,128)(2,1)S(1)}, bf16[320,512]{1,0:T(8,128)(2,1)S(1)}, u32[]{:S(2)}, u32[]{:S(2)}) %collective-permute-start.8) | collective-permute-done | bytes 327712 | tf_op jit(solution)/shard_map/ppermute | solution.py:388
  41.9 5.8 %edge.1 = bf16[4,2,6,24,512]{4,3,2,1,0:T(8,128)(2,1)} custom-call(bf16[320,512]{1,0:T(8,128)(2,1)S(1)} %collective-permute-done.7.first, bf16[320,512]{1,0:T(8,128)(2,1)S(1)} %collective-permute-done.8.second, bf16[2,2,80,256]{3,2,1,0:T(8,128)(2,1)S(1)} %get-tuple-element.62.key_a, bf16[2,2,80,256]{3,2,1,0:T(8,128)(2,1)S(1)} %get-tuple-element.63.value_a, ...), custom_call_target="tpu_custom_call" | custom-call | flops 4000000000 | bytes 2097152 | tf_op jit(solution)/shard_map/edge/pallas_call | solution.py:470
  (3 shorter events, 0.1 us)
Async XLA Ops:
  0.0 18.5 %copy-start.8 = (s32[1,1232]{1,0:T(1,128)S(1)}, s32[1,1232]{1,0:T(1,128)}, u32[]{:S(2)}) copy-start(s32[1,1232]{1,0:T(1,128)} %constant.19) | copy-start | bytes 14788
  0.0 18.5 %copy-start.9 = (s32[1,1232]{1,0:T(1,128)S(1)}, s32[1,1232]{1,0:T(1,128)}, u32[]{:S(2)}) copy-start(s32[1,1232]{1,0:T(1,128)} %constant.20) | copy-start | bytes 14788
  3.7 16.1 %copy-start.4 = (bf16[592,512]{1,0:T(8,128)(2,1)S(1)}, bf16[592,512]{1,0:T(8,128)(2,1)}, u32[]{:S(2)}) copy-start(bf16[592,512]{1,0:T(8,128)(2,1)} %get-tuple-element.37.norm_b) | copy-start | bytes 1818628
  3.7 16.1 %copy-start.5 = (bf16[592,512]{1,0:T(8,128)(2,1)S(1)}, bf16[592,512]{1,0:T(8,128)(2,1)}, u32[]{:S(2)}) copy-start(bf16[592,512]{1,0:T(8,128)(2,1)} %get-tuple-element.40.norm_a) | copy-start | bytes 1818628
  3.7 16.1 %copy-start.7 = (bf16[2304,128]{1,0:T(8,128)(2,1)S(1)}, bf16[2304,128]{1,0:T(8,128)(2,1)}, u32[]{:S(2)}) copy-start(bf16[2304,128]{1,0:T(8,128)(2,1)} %get-tuple-element.41.refs_0_) | copy-start | bytes 1769476
  3.7 14.8 %collective-permute-start.2 = (bf16[1152,128]{1,0:T(8,128)(2,1)}, bf16[1152,128]{1,0:T(8,128)(2,1)S(1)}, u32[]{:S(2)}, u32[]{:S(2)}) collective-permute-start(bf16[1152,128]{1,0:T(8,128)(2,1)} %get-tuple-element.50), channel_id=1, source_target_pairs={{0,2},{1,3},{2,128},{3,129},{4,6},{5,7},{6,132},{7,133},{8,10},{9,... | collective-permute-start | bytes 884744 | tf_op jit(solution)/shard_map/ppermute | solution.py:388
  5.9 13.2 %collective-permute-start.3 = (bf16[1152,128]{1,0:T(8,128)(2,1)}, bf16[1152,128]{1,0:T(8,128)(2,1)}, u32[]{:S(2)}, u32[]{:S(2)}) collective-permute-start(bf16[1152,128]{1,0:T(8,128)(2,1)} %get-tuple-element.51), channel_id=1, source_target_pairs={{0,130},{1,131},{2,0},{3,1},{4,134},{5,135},{6,4},{7,5},{8,138},{9... | collective-permute-start | bytes 884744 | tf_op jit(solution)/shard_map/ppermute | solution.py:388
  7.5 12.3 %collective-permute-start.1 = (bf16[2304,128]{1,0:T(8,128)(2,1)}, bf16[2304,128]{1,0:T(8,128)(2,1)}, u32[]{:S(2)}, u32[]{:S(2)}) collective-permute-start(bf16[2304,128]{1,0:T(8,128)(2,1)} %get-tuple-element.41.refs_0_), channel_id=1, source_target_pairs={{0,1},{1,0},{2,3},{3,2},{4,5},{5,4},{6,7},{7,6},{8,9},{9,8},{10,11... | collective-permute-start | bytes 1769480 | tf_op jit(solution)/shard_map/ppermute | solution.py:388
  10.3 15.8 %collective-permute-start = (bf16[592,512]{1,0:T(8,128)(2,1)}, bf16[592,512]{1,0:T(8,128)(2,1)S(1)}, u32[]{:S(2)}, u32[]{:S(2)}) collective-permute-start(bf16[592,512]{1,0:T(8,128)(2,1)} %get-tuple-element.37.norm_b), channel_id=1, source_target_pairs={{0,4},{1,5},{2,6},{3,7},{4,0},{5,1},{6,2},{7,3},{8,12},{9,13},{10,... | collective-permute-start | bytes 1818632 | tf_op jit(solution)/shard_map/ppermute | solution.py:388
  10.3 22.2 %collective-permute-start.6 = (bf16[592,512]{1,0:T(8,128)(2,1)}, bf16[592,512]{1,0:T(8,128)(2,1)S(1)}, u32[]{:S(2)}, u32[]{:S(2)}) collective-permute-start(bf16[592,512]{1,0:T(8,128)(2,1)} %get-tuple-element.40.norm_a), channel_id=1, source_target_pairs={{0,252},{1,253},{2,254},{3,255},{4,8},{5,9},{6,10},{7,11},{8,4},{9... | collective-permute-start | bytes 1818632 | tf_op jit(solution)/shard_map/ppermute | solution.py:388
  18.5 4.7 %collective-permute-start.4 = (bf16[1152,128]{1,0:T(8,128)(2,1)S(1)}, bf16[1152,128]{1,0:T(8,128)(2,1)S(1)}, u32[]{:S(2)}, u32[]{:S(2)}) collective-permute-start(bf16[1152,128]{1,0:T(8,128)(2,1)S(1)} %collective-permute-done.2.refs_0_), channel_id=1, source_target_pairs={{0,1},{1,0},{2,3},{3,2},{4,5},{5,4},{6,7},{7,6},{8,9},{9,8},{10,11... | collective-permute-start | bytes 884744 | tf_op jit(solution)/shard_map/ppermute | solution.py:388
  19.2 4.1 %collective-permute-start.5 = (bf16[1152,128]{1,0:T(8,128)(2,1)}, bf16[1152,128]{1,0:T(8,128)(2,1)S(1)}, u32[]{:S(2)}, u32[]{:S(2)}) collective-permute-start(bf16[1152,128]{1,0:T(8,128)(2,1)} %collective-permute-done.3.refs_1_), channel_id=1, source_target_pairs={{0,1},{1,0},{2,3},{3,2},{4,5},{5,4},{6,7},{7,6},{8,9},{9,8},{10,11... | collective-permute-start | bytes 884744 | tf_op jit(solution)/shard_map/ppermute | solution.py:388
  19.8 3.1 %copy-start = (bf16[512,2048]{1,0:T(8,128)(2,1)S(1)}, bf16[512,2048]{1,0:T(8,128)(2,1)}, u32[]{:S(2)}) copy-start(bf16[512,2048]{1,0:T(8,128)(2,1)} %up_in.1) | copy-start | bytes 6291460
  19.8 3.1 %copy-start.1 = (bf16[2048,512]{1,0:T(8,128)(2,1)S(1)}, bf16[2048,512]{1,0:T(8,128)(2,1)}, u32[]{:S(2)}) copy-start(bf16[2048,512]{1,0:T(8,128)(2,1)} %down_in.1) | copy-start | bytes 6291460
  23.2 2.9 %copy-start.2 = (f32[592,512]{1,0:T(8,128)S(1)}, f32[592,512]{1,0:T(8,128)}, u32[]{:S(2)}) copy-start(f32[592,512]{1,0:T(8,128)} %get-tuple-element.38.resid.resid_b) | copy-start | bytes 3637252
  23.2 2.9 %copy-start.6 = (f32[1,512]{1,0:T(1,128)S(1)}, f32[1,512]{1,0:T(1,128)}, u32[]{:S(2)}) copy-start(f32[1,512]{1,0:T(1,128)} %get-tuple-element.39.gain) | copy-start | bytes 6148
  32.5 3.5 %copy-start.3 = (f32[592,512]{1,0:T(8,128)S(1)}, f32[592,512]{1,0:T(8,128)}, u32[]{:S(2)}) copy-start(f32[592,512]{1,0:T(8,128)} %get-tuple-element.61.resid.resid_a) | copy-start | bytes 3637252
  32.6 8.1 %collective-permute-start.7 = (bf16[320,512]{1,0:T(8,128)(2,1)S(1)}, bf16[320,512]{1,0:T(8,128)(2,1)S(1)}, u32[]{:S(2)}, u32[]{:S(2)}) collective-permute-start(bf16[320,512]{1,0:T(8,128)(2,1)S(1)} %get-tuple-element.59), channel_id=1, source_target_pairs={{0,1},{1,0},{2,3},{3,2},{4,5},{5,4},{6,7},{7,6},{8,9},{9,8},{10,11... | collective-permute-start | bytes 983048 | tf_op jit(solution)/shard_map/ppermute | solution.py:388
  33.5 8.4 %collective-permute-start.8 = (bf16[320,512]{1,0:T(8,128)(2,1)S(1)}, bf16[320,512]{1,0:T(8,128)(2,1)S(1)}, u32[]{:S(2)}, u32[]{:S(2)}) collective-permute-start(bf16[320,512]{1,0:T(8,128)(2,1)S(1)} %get-tuple-element.60), channel_id=1, source_target_pairs={{1,2},{2,1},{5,6},{6,5},{9,10},{10,9},{13,14},{14,13},{17,18},{18,... | collective-permute-start | bytes 983048 | tf_op jit(solution)/shard_map/ppermute | solution.py:388
